TPU v7x, 32 devices: a whole 2x2x4 slice. The times are simulated.
32 devices in a mesh: gx: 4 (over x, core), gy: 4 (over z), gz: 2 (over y).
Axes of the slice: x: 2, y: 2, z: 4, core: 2. Of those that a mesh axis runs over, the one named last changes fastest.
Arguments:
- species: float32 [4, 64, 128, 256], P(None, 'gx', 'gy', 'gz'), may hold values from -6 to 6
- velocity: float32 [3, 64, 128, 256], P(None, 'gx', 'gy', 'gz'), may hold values from -15 to 15
- diffusivity: float32 [64, 128, 256], P('gx', 'gy', 'gz'), may hold values from 0.05 to 1
- reaction: float32 [4, 4], replicated, may hold values from -8 to 8
Outputs:
- updated: float32 [4, 64, 128, 256], P(None, 'gx', 'gy', 'gz')
- gram: float32 [256, 256], P('gx', 'gz')
All inputs are finite; a program needn't handle non-finite values. Where the computation divides by a largest or mean magnitude, that divisor is 1e-20 or more.
Results may differ from a plain program's by a relative error of at most 0.000068.
Values sent between devices are 32-bit elements; how exact they have to be, the bound alone decides.
A program may use at most 64 MiB of HBM per device.

v0:
```python
import jax
import jax.numpy as jnp
from jax import lax
from jax.sharding import PartitionSpec as P

first_coeffs = (4.0 / 5.0, -1.0 / 5.0, 4.0 / 105.0, -1.0 / 280.0)
second_coeffs = (8.0 / 5.0, -1.0 / 5.0, 8.0 / 315.0, -1.0 / 560.0)
centre_weight = -205.0 / 72.0
courant = 0.8


def extended(x, sides, width):
    for axis, dim in sides:
        peers, length = (lax.axis_size(axis), x.shape[dim])
        up = [(i, (i + 1) % peers) for i in range(peers)]
        down = [(j, i) for i, j in up]
        last = lax.slice_in_dim(x, length - width, length, axis=dim)
        initial = lax.slice_in_dim(x, 0, width, axis=dim)
        before = lax.ppermute(last, axis, up)
        after = lax.ppermute(initial, axis, down)
        x = jnp.concatenate([before, x, after], axis=dim)
    return x


def neighbour(padded, dimension, offset, cells_x, cells_y, cells_z):
    lows = [4, 4, 4]
    lows[dimension - 1] = 4 + offset
    return padded[
        :, lows[0] : lows[0] + cells_x, lows[1] : lows[1] + cells_y, lows[2] : lows[2] + cells_z
    ]


def body(species, velocity, diffusivity, reaction):
    local_speed = jnp.max(jnp.abs(velocity[0]) + jnp.abs(velocity[1]) + jnp.abs(velocity[2]))
    fastest = lax.pmax(local_speed, ("gx", "gy", "gz"))
    time_step = courant / fastest
    padded = extended(species, (("gx", 1), ("gy", 2), ("gz", 3)), 4)
    cells_x, cells_y, cells_z = (species.shape[1], species.shape[2], species.shape[3])
    tendency = jnp.einsum("kj,jxyz->kxyz", reaction, species, precision=lax.Precision.HIGHEST)
    for direction in range(3):
        dimension = direction + 1
        first_der = jnp.zeros_like(species)
        second_der = centre_weight * species
        for reach in range(1, 5):
            ahead = neighbour(padded, dimension, reach, cells_x, cells_y, cells_z)
            behind = neighbour(padded, dimension, -reach, cells_x, cells_y, cells_z)
            first_der = first_der + first_coeffs[reach - 1] * (ahead - behind)
            second_der = second_der + second_coeffs[reach - 1] * (ahead + behind)
        tendency = tendency - velocity[direction] * first_der + diffusivity * second_der
    updated = species + time_step * tendency
    nspec = species.shape[0]
    unfolding = jnp.transpose(updated, (1, 0, 2, 3)).reshape(cells_x * nspec, cells_y * cells_z)
    partial_gram = jnp.dot(
        unfolding,
        lax.all_gather(unfolding, "gx", axis=0, tiled=True).T,
        precision=lax.Precision.HIGHEST,
        preferred_element_type=jnp.float32,
    )
    count_y = lax.axis_size("gy")
    count_z = lax.axis_size("gz")
    column_part = lax.psum_scatter(partial_gram, "gz", scatter_dimension=1, tiled=True)
    summed = lax.psum(column_part, "gy")
    columns_all = float(cells_y * cells_z * count_y * count_z)
    gram = summed / columns_all
    return (updated, gram)


def solution(mesh):
    placed = (P(None, "gx", "gy", "gz"), P(None, "gx", "gy", "gz"), P("gx", "gy", "gz"), P())
    return jax.shard_map(
        body,
        mesh=mesh,
        in_specs=placed,
        out_specs=(P(None, "gx", "gy", "gz"), P("gx", "gz")),
        check_vma=False,
    )
```

profile of v0, /device:TPU:0, one launch (start us, length us, event | category | flops | bytes accessed | tf_op | source)
XLA Modules:
  0.0 190.8 jit_solution(10716245312543087192)
XLA Ops:
  7.2 0.0 copy-start
  7.2 0.0 copy-start.2
  7.2 0.0 all-gather.2.cloned.1.call-start
  7.2 1.2 fusion.22
  8.4 0.2 copy.48
  8.6 0.5 collective-permute-start.1
  9.1 0.2 copy.49
  9.3 2.0 %collective-permute-start = (f32[4,4,32,128]{3,0,2,1:T(4,128)S(1)}, f32[4,4,32,128]{3,0,2,1:T(4,128)S(1)}, u32[]{:S(2)}, u32[]{:S(2)}) collective-permute-start(f32[4,4,32,128]{3,0,2,1:T(4,128)S(1)} %copy.49), channel_id=1, source_target_pairs={{8,0},{16,8},{24,16},{0,24},{9,1},{17,9},{25,17},{1,25},{10,2},{18... | collective-permute-start | bytes 786440 | tf_op jit(solution)/shard_map/ppermute | solution.py:20
  11.3 3.8 %collective-permute-done.1 = f32[4,4,32,128]{3,0,2,1:T(4,128)S(1)} collective-permute-done((f32[4,4,32,128]{3,0,2,1:T(4,128)S(1)}, f32[4,4,32,128]{3,0,2,1:T(4,128)S(1)}, u32[]{:S(2)}, u32[]{:S(2)}) %collective-permute-start.1) | collective-permute-done | bytes 262176 | tf_op jit(solution)/shard_map/ppermute | solution.py:19
  15.1 0.1 constant_dynamic-update-slice_fusion.3
  15.1 0.0 copy-start.1
  15.2 1.1 constant_dynamic-update-slice_fusion.1
  16.3 1.4 collective-permute-done
  17.7 0.1 constant_dynamic-update-slice_fusion
  17.8 3.8 %collective-permute-start.2 = (f32[4,24,4,128]{3,0,2,1:T(4,128)S(1)}, f32[4,24,4,128]{3,0,2,1:T(4,128)S(1)}, u32[]{:S(2)}, u32[]{:S(2)}) collective-permute-start(f32[4,24,4,128]{3,0,2,1:T(4,128)S(1)} %get-tuple-element.13), channel_id=1, source_target_pairs={{2,0},{4,2},{6,4},{0,6},{3,1},{5,3},{7,5},{1,7},{10,8},{12,10},{14... | collective-permute-start | bytes 589832 | tf_op jit(solution)/shard_map/ppermute | solution.py:20
  21.6 0.0 collective-permute-start.3
  21.6 0.0 copy-done.1
  21.6 0.7 add_reduce_fusion
  22.3 4.7 %collective-permute-done.2 = f32[4,24,4,128]{3,0,2,1:T(4,128)S(1)} collective-permute-done((f32[4,24,4,128]{3,0,2,1:T(4,128)S(1)}, f32[4,24,4,128]{3,0,2,1:T(4,128)S(1)}, u32[]{:S(2)}, u32[]{:S(2)}) %collective-permute-start.2) | collective-permute-done | bytes 196640 | tf_op jit(solution)/shard_map/ppermute | solution.py:20
  27.0 0.0 copy-done.8
  27.0 4.8 %collective-permute-done.3 = f32[4,24,4,128]{3,0,2,1:T(4,128)S(1)} collective-permute-done((f32[4,24,4,128]{3,0,2,1:T(4,128)S(1)}, f32[4,24,4,128]{3,0,2,1:T(4,128)S(1)}, u32[]{:S(2)}, u32[]{:S(2)}) %collective-permute-start.3) | collective-permute-done | bytes 196640 | tf_op jit(solution)/shard_map/ppermute | solution.py:19
  31.8 0.7 copy-done.7
  32.4 0.5 pad_maximum_fusion.1
  32.9 2.5 %fusion.20 = (f32[4,24,40,4]{3,0,2,1:T(4,128)}, f32[4,24,40,4]{3,0,2,1:T(4,128)S(1)}) fusion(f32[4,24,40,128]{3,0,2,1:T(4,128)S(1)} %pad_maximum_fusion.1), kind=kLoop, calls=%fused_computation.52 | loop fusion | bytes 245760 | tf_op jit(solution)/shard_map/slice | solution.py:18
  35.4 3.0 %copy.32 = f32[4,24,40,4]{2,1,3,0:T(8,128)} copy(f32[4,24,40,4]{3,0,2,1:T(4,128)} %get-tuple-element.10) | data formatting | bytes 122880 | tf_op jit(solution)/shard_map/slice | solution.py:18
  38.4 1.5 collective-permute-start.4
  39.9 2.1 %copy.34 = f32[4,24,40,4]{2,1,3,0:T(8,128)} copy(f32[4,24,40,4]{3,0,2,1:T(4,128)S(1)} %get-tuple-element.11) | data formatting | bytes 122880 | tf_op jit(solution)/shard_map/slice | solution.py:17
  42.0 0.5 collective-permute-start.5
  42.5 2.0 %slice_bitcast_fusion.2 = (f32[16,32,128]{2,1,0:T(8,128)}, f32[16,32,128]{2,1,0:T(8,128)}, f32[16,32,128]{2,1,0:T(8,128)}) fusion(f32[3,16,32,128]{3,2,1,0:T(8,128)} %param.5), kind=kLoop, calls=%fused_computation.40 | loop fusion | bytes 1572864 | tf_op jit(solution)/shard_map/squeeze | solution.py:34
  44.6 40.5 %pmax.7 = f32[]{:T(128)} all-reduce(f32[]{:T(128)} %add_reduce_fusion), channel_id=1, replica_groups=mesh['gx'=4,'gy'=4,'gz'=2] {'gx','gy','gz'}, use_global_device_ids=true, to_apply=%region_1.0 | all-reduce | flops 1 | bytes 8 | tf_op jit(solution)/shard_map/pmax | solution.py:35
  85.8 0.0 collective-permute-done.4
  85.8 2.4 %copy.33 = f32[4,24,40,4]{3,0,2,1:T(4,128)S(1)} copy(f32[4,24,40,4]{2,1,3,0:T(8,128)} %collective-permute-done.4) | data formatting | bytes 122880 | tf_op jit(solution)/shard_map/ppermute | solution.py:20
  88.2 0.0 collective-permute-done.5
  88.2 2.8 %copy.35 = f32[4,24,40,4]{3,0,2,1:T(4,128)} copy(f32[4,24,40,4]{2,1,3,0:T(8,128)} %collective-permute-done.5) | data formatting | bytes 122880 | tf_op jit(solution)/shard_map/ppermute | solution.py:19
  91.0 6.8 %pad_maximum_fusion = (f32[4,24,40,132]{3,0,2,1:T(4,128)S(1)}, f32[4,24,40,132]{3,0,2,1:T(4,128)}) fusion(f32[4,24,40,4]{3,0,2,1:T(4,128)S(1)} %copy.33, f32[4,24,4,128]{3,0,2,1:T(4,128)} %copy-done.6, f32[4,24,32,128]{3,0,2,1:T(4,128)S(1)} %get-tuple-element.23, f32[4,24,4,128]{3,0,2,1:T(4,128)} %copy-done.7, f32[4,24,40,4]{3,0,2,1:T(4,128)} %copy.35), kind=kLoop, calls=%fused_computation | loop fusion | flops 3041280 | bytes 6144000 | tf_op jit(solution)/shard_map/concatenate | solution.py:21
  97.8 0.0 copy-done.3
  97.8 13.3 %fusion.6 = f32[4,16,32,128]{3,0,2,1:T(4,128)S(1)} fusion(f32[4,24,40,132]{3,0,2,1:T(4,128)} %get-tuple-element.9, f32[4,24,40,132]{3,0,2,1:T(4,128)S(1)} %get-tuple-element.8, f32[4,24,4,128]{3,0,2,1:T(4,128)} %copy-done.6, f32[4,24,32,128]{3,0,2,1:T(4,128)S(1)} %get-tuple-element.23, f32[4,24,4,128]{3,0,2,1:T(4,128)} %copy-done.7, ...), kind=kOutput, calls=%fused_computation.22 | convolution fusion | flops 36700160 | bytes 22939652 | tf_op jit(solution)/shard_map/kj,jxyz->kxyz/dot_general | solution.py:39
  111.1 0.1 copy.37
  111.2 1.6 copy.50
  112.8 0.0 all-gather.2.cloned.1.call-update
  112.9 0.2 reduce-scatter.2.cloned.1.call-start
  113.1 33.7 %all-gather.2.cloned.1.call-done = f32[256,4096]{1,0:T(8,128)} async-done(((f32[64,4096]{1,0:T(8,128)}), f32[256,4096]{1,0:T(8,128)}) %all-gather.2.cloned.1.call-update) | async-done | bytes 4194320 | tf_op jit(solution)/shard_map/all_gather | solution.py:55
  146.8 6.9 %fusion.18 = f32[64,256]{1,0:T(8,128)} fusion(f32[256,4096]{1,0:T(8,128)} %all-gather.2.cloned.1.call-done, f32[8,8,32,128]{3,2,1,0:T(8,128)S(1)} %bitcast.26), kind=kOutput, calls=%fused_computation.50 | convolution fusion | flops 805306368 | bytes 5308416 | tf_op jit(solution)/shard_map/dot_general | solution.py:53
  153.6 0.0 reduce-scatter.2.cloned.1.call-update
  153.6 1.1 copy.38
  154.8 8.9 %reduce-scatter.2.cloned.1.call-done = f32[64,128]{1,0:T(8,128)} async-done(((f32[64,256]{1,0:T(8,128)}), f32[64,128]{1,0:T(8,128)}) %reduce-scatter.2.cloned.1.call-update) | async-done | bytes 32784 | tf_op jit(solution)/shard_map/reduce_scatter | solution.py:61
  163.7 19.6 %psum.7 = f32[64,128]{1,0:T(8,128)S(1)} all-reduce(f32[64,128]{1,0:T(8,128)} %reduce-scatter.2.cloned.1.call-done), channel_id=1, replica_groups=mesh['gx'=4,'gy'=4,'gz'=2] {'gy'}, use_global_device_ids=true, to_apply=%region_3.0 | all-reduce | flops 8192 | bytes 65536 | tf_op jit(solution)/shard_map/psum | solution.py:62
  183.3 0.6 broadcast_multiply_fusion
  (12 shorter events, 0.0 us)
Async XLA Ops:
  7.2 90.7 %copy-start = (f32[4,4]{1,0:T(4,128)S(1)}, f32[4,4]{1,0:T(4,128)}, u32[]{:S(2)}) copy-start(f32[4,4]{1,0:T(4,128)} %param.7) | copy-start | bytes 196
  7.2 8.0 %copy-start.2 = (f32[4,16,32,128]{3,2,1,0:T(8,128)S(1)}, f32[4,16,32,128]{3,2,1,0:T(8,128)}, u32[]{:S(2)}) copy-start(f32[4,16,32,128]{3,2,1,0:T(8,128)} %param.4) | copy-start | bytes 3145732
  7.2 139.6 %all-gather.2.cloned.1.call-start = ((), (), s32[]{:S(2)}) async-start(), calls=%async_computation.1 | async-start | bytes 5242880 | tf_op jit(solution)/shard_map/all_gather | solution.py:55
  8.6 6.5 %collective-permute-start.1 = (f32[4,4,32,128]{3,0,2,1:T(4,128)S(1)}, f32[4,4,32,128]{3,0,2,1:T(4,128)S(1)}, u32[]{:S(2)}, u32[]{:S(2)}) collective-permute-start(f32[4,4,32,128]{3,0,2,1:T(4,128)S(1)} %copy.48), channel_id=1, source_target_pairs={{0,8},{8,16},{16,24},{24,0},{1,9},{9,17},{17,25},{25,1},{2,10},{10... | collective-permute-start | bytes 786440 | tf_op jit(solution)/shard_map/ppermute | solution.py:19
  9.3 8.4 %collective-permute-start = (f32[4,4,32,128]{3,0,2,1:T(4,128)S(1)}, f32[4,4,32,128]{3,0,2,1:T(4,128)S(1)}, u32[]{:S(2)}, u32[]{:S(2)}) collective-permute-start(f32[4,4,32,128]{3,0,2,1:T(4,128)S(1)} %copy.49), channel_id=1, source_target_pairs={{8,0},{16,8},{24,16},{0,24},{9,1},{17,9},{25,17},{1,25},{10,2},{18... | collective-permute-start | bytes 786440 | tf_op jit(solution)/shard_map/ppermute | solution.py:20
  15.1 6.5 %copy-start.1 = (f32[3,16,32,128]{3,2,1,0:T(8,128)S(1)}, f32[3,16,32,128]{3,2,1,0:T(8,128)}, u32[]{:S(2)}) copy-start(f32[3,16,32,128]{3,2,1,0:T(8,128)} %param.5) | copy-start | bytes 2359300
  16.3 10.7 %copy-start.8 = (f32[4,20,32,128]{3,0,2,1:T(4,128)}, f32[4,20,32,128]{3,0,2,1:T(4,128)S(1)}, u32[]{:S(2)}) copy-start(f32[4,20,32,128]{3,0,2,1:T(4,128)S(1)} %get-tuple-element.16) | copy-start | bytes 3932164
  17.8 9.2 %copy-start.4 = (f32[4,20,32,128]{3,0,2,1:T(4,128)}, f32[4,20,32,128]{3,0,2,1:T(4,128)S(1)}, u32[]{:S(2)}) copy-start(f32[4,20,32,128]{3,0,2,1:T(4,128)S(1)} %get-tuple-element.22) | copy-start | bytes 3932164
  17.8 9.1 %collective-permute-start.2 = (f32[4,24,4,128]{3,0,2,1:T(4,128)S(1)}, f32[4,24,4,128]{3,0,2,1:T(4,128)S(1)}, u32[]{:S(2)}, u32[]{:S(2)}) collective-permute-start(f32[4,24,4,128]{3,0,2,1:T(4,128)S(1)} %get-tuple-element.13), channel_id=1, source_target_pairs={{2,0},{4,2},{6,4},{0,6},{3,1},{5,3},{7,5},{1,7},{10,8},{12,10},{14... | collective-permute-start | bytes 589832 | tf_op jit(solution)/shard_map/ppermute | solution.py:20
  21.6 10.1 %collective-permute-start.3 = (f32[4,24,4,128]{3,0,2,1:T(4,128)S(1)}, f32[4,24,4,128]{3,0,2,1:T(4,128)S(1)}, u32[]{:S(2)}, u32[]{:S(2)}) collective-permute-start(f32[4,24,4,128]{3,0,2,1:T(4,128)S(1)} %get-tuple-element.12), channel_id=1, source_target_pairs={{0,2},{2,4},{4,6},{6,0},{1,3},{3,5},{5,7},{7,1},{8,10},{10,12},{12... | collective-permute-start | bytes 589832 | tf_op jit(solution)/shard_map/ppermute | solution.py:19
  27.0 4.8 %copy-start.6 = (f32[4,24,4,128]{3,0,2,1:T(4,128)}, f32[4,24,4,128]{3,0,2,1:T(4,128)S(1)}, u32[]{:S(2)}) copy-start(f32[4,24,4,128]{3,0,2,1:T(4,128)S(1)} %collective-permute-done.2) | copy-start | bytes 589828
  31.8 0.7 copy-start.7
  38.4 47.3 %collective-permute-start.4 = (f32[4,24,40,4]{2,1,3,0:T(8,128)}, f32[4,24,40,4]{2,1,3,0:T(8,128)}, u32[]{:S(2)}, u32[]{:S(2)}) collective-permute-start(f32[4,24,40,4]{2,1,3,0:T(8,128)} %copy.32), channel_id=1, source_target_pairs={{1,0},{0,1},{3,2},{2,3},{5,4},{4,5},{7,6},{6,7},{9,8},{8,9},{11,10... | collective-permute-start | bytes 184328 | tf_op jit(solution)/shard_map/ppermute | solution.py:20
  42.0 46.2 %collective-permute-start.5 = (f32[4,24,40,4]{2,1,3,0:T(8,128)}, f32[4,24,40,4]{2,1,3,0:T(8,128)}, u32[]{:S(2)}, u32[]{:S(2)}) collective-permute-start(f32[4,24,40,4]{2,1,3,0:T(8,128)} %copy.34), channel_id=1, source_target_pairs={{0,1},{1,0},{2,3},{3,2},{4,5},{5,4},{6,7},{7,6},{8,9},{9,8},{10,11... | collective-permute-start | bytes 184328 | tf_op jit(solution)/shard_map/ppermute | solution.py:19
  91.0 6.8 %copy-start.3 = (f32[4,16,32,128]{3,2,1,0:T(8,128)S(1)}, f32[4,16,32,128]{3,2,1,0:T(8,128)}, u32[]{:S(2)}) copy-start(f32[4,16,32,128]{3,2,1,0:T(8,128)} %param.4) | copy-start | bytes 3145732
  91.0 6.8 %copy-start.5 = (f32[4,20,32,128]{3,0,2,1:T(4,128)S(1)}, f32[4,20,32,128]{3,0,2,1:T(4,128)}, u32[]{:S(2)}) copy-start(f32[4,20,32,128]{3,0,2,1:T(4,128)} %copy-done.4) | copy-start | bytes 3932164
  112.9 50.8 %reduce-scatter.2.cloned.1.call-start = ((), (), s32[]{:S(2)}) async-start(), calls=%async_computation.2 | async-start | bytes 98304 | tf_op jit(solution)/shard_map/reduce_scatter | solution.py:61
Sparse Core Ops, SparseCore 0:
  113.0 33.7 all-gather.1
  153.8 9.8 reduce-scatter.1
where the time goes:
time: 191 us
  blocking collectives  60.1 us (31%)
  waiting for transfers between devices  57.3 us (30%)
  local copies, waits for them, and re-layouts  21.2 us (11%)
  matrix products  20.1 us (11%)
  between operations  14.9 us (8%)
  starting transfers between devices  8.58 us (4%)
  other arithmetic  8.58 us (4%)
    pmax x1, blocking collectives, body(): fastest = lax.pmax(local_speed, ('gx', 'gy', 'gz'))  40.5 us
    all_gather x1, waiting for transfers between devices, body(): lax.all_gather(unfolding, 'gx', axis=0, tiled=True)  33.7 us
    psum x1, blocking collectives, body(): summed = lax.psum(column_part, 'gy')  19.6 us
    dot_general x1, matrix products, body(): jnp.einsum('kj,jxyz->kxyz', reaction, species, precision=lax.Precision.HI...  13.3 us
    reduce_scatter x1, waiting for transfers between devices, body(): lax.psum_scatter(partial_gram, 'gz', scatter_dimension=1, tiled=True)  8.93 us
    ppermute x3, waiting for transfers between devices, extended(): before = lax.ppermute(last, axis, up)  8.58 us
    ppermute x3, starting transfers between devices, extended(): after = lax.ppermute(initial, axis, down)  7.31 us
    concatenate x2, other arithmetic, extended(): x = jnp.concatenate([before, x, after], axis=dim)  7.28 us
  transfers between devices with their start and end apart: 8, of which 6 were waited for; matrix products, arithmetic and copies ran while one was open for 5% of the time, Pallas kernels for 0%

commit v1 on v0

v1 whole, which is shorter than its diff:
```python
import functools

import jax
import jax.numpy as jnp
import numpy as np
from jax import lax
from jax.experimental import pallas as pl
from jax.experimental.pallas import tpu as pltpu
from jax.sharding import PartitionSpec as P

first_coeffs = (4.0 / 5.0, -1.0 / 5.0, 4.0 / 105.0, -1.0 / 280.0)
second_coeffs = (8.0 / 5.0, -1.0 / 5.0, 8.0 / 315.0, -1.0 / 560.0)
centre_weight = -205.0 / 72.0
courant = 0.8
MESH = pl.DeviceIdType.MESH
HIGHEST = lax.Precision.HIGHEST


def lane_matrix(lanes):
    place = np.arange(lanes)
    halo = np.where(place < lanes // 2, place + lanes, place - lanes)
    rows = np.concatenate([place, halo])
    offset = rows[:, None] - place[None, :]
    first = np.zeros(offset.shape)
    second = np.where(offset == 0, 3.0 * centre_weight, 0.0)
    for reach in range(1, 5):
        a, b = first_coeffs[reach - 1], second_coeffs[reach - 1]
        first += a * (offset == reach) - a * (offset == -reach)
        second += b * ((offset == reach) | (offset == -reach))
    return np.concatenate([first, second], axis=1).astype(np.float32)


def kernel(
    sizes, columns_all, sp, vel, dif, reac, lane_mat, out, gram,
    pad, v, d, tend, uout, usend, ufull, zsend, zrecv, msend, mrecv,
    gpart, garecv, gbsend, gbrecv, gcall,
    load_sem, out_sem, own_sem, hs, hr, ms, mr, us, ur, gas, gar, gbs, gbr, gcs, gcr,
):
    count_x, count_y, count_z = sizes
    kinds, nx, ny, lanes = sp.shape
    axes = ("gx", "gy", "gz")
    here = {a: lax.axis_index(a) for a in axes}

    def peer(axis, step):
        n = sizes[axes.index(axis)]
        return {axis: lax.rem(here[axis] + step + n, n)}

    def send(src, dst, s, r, device):
        copy = pltpu.make_async_remote_copy(
            src_ref=src, dst_ref=dst, send_sem=s, recv_sem=r, device_id=device, device_id_type=MESH
        )
        copy.start()
        return copy

    barrier = pltpu.get_barrier_semaphore()
    for axis, n in zip(axes, sizes):
        for step in range(1, n):
            pl.semaphore_signal(barrier, inc=1, device_id=peer(axis, step), device_id_type=MESH)
    loads = [
        pltpu.make_async_copy(vel, v, load_sem.at[0]),
        pltpu.make_async_copy(sp, pad.at[:, 4 : 4 + nx, 8 : 8 + ny, :], load_sem.at[1]),
        pltpu.make_async_copy(dif, d, load_sem.at[2]),
    ]
    for c in loads:
        c.start()
    pl.semaphore_wait(barrier, count_x + count_y + count_z - 3)

    x_halo = [
        send(sp.at[:, nx - 4 :], pad.at[:, 0:4, 8 : 8 + ny, :], hs.at[0], hr.at[0], peer("gx", 1)),
        send(sp.at[:, 0:4], pad.at[:, 4 + nx : 8 + nx, 8 : 8 + ny, :], hs.at[1], hr.at[1], peer("gx", -1)),
    ]
    y_halo = [
        send(sp.at[:, :, ny - 4 :], pad.at[:, 4 : 4 + nx, 4:8, :], hs.at[2], hr.at[2], peer("gy", 1)),
        send(sp.at[:, :, 0:4], pad.at[:, 4 : 4 + nx, 8 + ny : 12 + ny, :], hs.at[3], hr.at[3], peer("gy", -1)),
    ]

    loads[0].wait()

    def speed(x, m):
        s = jnp.abs(v[0, x]) + jnp.abs(v[1, x]) + jnp.abs(v[2, x])
        return jnp.maximum(m, jnp.max(s.reshape(ny // 8, 8, lanes), axis=0))

    most = lax.fori_loop(0, nx, speed, jnp.zeros((8, lanes), jnp.float32))

    def max_start(stage, value):
        n = sizes[stage]
        msend[stage] = value
        return [
            send(msend.at[stage], mrecv.at[stage, k - 1], ms.at[stage, k - 1], mr.at[stage, k - 1], peer(axes[stage], k))
            for k in range(1, n)
        ]

    def max_end(stage, value, copies):
        for k, c in enumerate(copies):
            c.wait()
            value = jnp.maximum(value, mrecv[stage, k])
        return value

    stage_copies = max_start(0, most)

    loads[1].wait()
    lane = lax.broadcasted_iota(jnp.int32, (kinds * ny, lanes), 1)
    edge = (lane < 4) | (lane >= lanes - 4)

    def pack(x, total):
        s = pad[:, 4 + x, 8 : 8 + ny, :].reshape(kinds * ny, lanes)
        return total + pltpu.roll(jnp.where(edge, s, 0.0), 4 + 8 * x, 1)

    zsend[...] = lax.fori_loop(0, nx, pack, jnp.zeros((kinds * ny, lanes), jnp.float32))
    z_halo = [send(zsend, zrecv.at[0], hs.at[4], hr.at[4], peer("gz", 1))]
    if count_z > 2:
        z_halo.append(send(zsend, zrecv.at[1], hs.at[5], hr.at[5], peer("gz", -1)))

    most = max_end(0, most, stage_copies)
    stage_copies = max_start(1, most)

    loads[2].wait()
    for c in z_halo:
        c.wait()
    if count_z > 2:
        wide = lax.broadcasted_iota(jnp.int32, (kinds * ny, lanes), 1) % 8
        zsend[...] = jnp.where(wide < 4, zrecv[0], zrecv[1])
    else:
        zsend[...] = zrecv[0]
    most = max_end(1, most, stage_copies)
    stage_copies = max_start(2, most)
    for c in y_halo:
        c.wait()

    def rest(x, carry):
        s = pad[:, 4 + x, 8 : 8 + ny, :]
        halo = pltpu.roll(zsend[...], lanes - 4 - 8 * x, 1)
        both = jnp.concatenate([s.reshape(kinds * ny, lanes), halo], axis=1)
        along_z = jnp.dot(both, lane_mat[...], precision=HIGHEST, preferred_element_type=jnp.float32)
        z1 = along_z[:, :lanes].reshape(kinds, ny, lanes)
        z2 = along_z[:, lanes:].reshape(kinds, ny, lanes)
        vy, vz, dd = v[1, x], v[2, x], d[x]
        for k in range(kinds):
            first = jnp.zeros((ny, lanes), jnp.float32)
            second = z2[k]
            for r in range(1, 5):
                ahead = pad[k, 4 + x, 8 + r : 8 + ny + r, :]
                behind = pad[k, 4 + x, 8 - r : 8 + ny - r, :]
                first = first + first_coeffs[r - 1] * (ahead - behind)
                second = second + second_coeffs[r - 1] * (ahead + behind)
            t = dd * second - vy * first - vz * z1[k]
            for j in range(kinds):
                t = t + reac[k, j] * s[j]
            tend[k, x] = t
        return carry

    lax.fori_loop(0, nx, rest, 0)

    most = max_end(2, most, stage_copies)
    fastest = jnp.max(most, keepdims=True)
    dt = jnp.broadcast_to(courant / fastest, (ny, lanes))

    share = ny // count_x
    rows_all = count_x * nx * kinds

    def finish(x, carry):
        vx, dd = v[0, x], d[x]
        for k in range(kinds):
            first = jnp.zeros((ny, lanes), jnp.float32)
            second = jnp.zeros((ny, lanes), jnp.float32)
            for r in range(1, 5):
                ahead = pad[k, 4 + x + r, 8 : 8 + ny, :]
                behind = pad[k, 4 + x - r, 8 : 8 + ny, :]
                first = first + first_coeffs[r - 1] * (ahead - behind)
                second = second + second_coeffs[r - 1] * (ahead + behind)
            u = pad[k, 4 + x, 8 : 8 + ny, :] + dt * (tend[k, x] - vx * first + dd * second)
            uout[k, x] = u
            row = pl.multiple_of((x * kinds + k) * share, share)
            usend[:, pl.ds(row, share), :] = u.reshape(count_x, share, lanes)
        return carry

    me_x = here["gx"]
    pending, outs = [], []

    def chunk(index, low, high):
        lax.fori_loop(low, high, finish, 0)
        rows = pl.ds(low * kinds * share, (high - low) * kinds * share)
        start = pl.multiple_of(me_x * (nx * kinds * share) + low * kinds * share, share)
        there = ufull.at[pl.ds(start, (high - low) * kinds * share)]
        for k in range(1, count_x):
            to = peer("gx", k)
            pending.append(
                send(usend.at[to["gx"], rows], there, us.at[index, k - 1], ur.at[index, k - 1], to)
            )
        own = pltpu.make_async_copy(usend.at[me_x, rows], there, own_sem.at[index])
        keep = pltpu.make_async_copy(uout.at[:, low:high], out.at[:, low:high], out_sem.at[index])
        for c in (own, keep):
            c.start()
        pending.append(own)
        outs.append(keep)

    chunk(0, 4, nx - 4)
    x_halo[0].wait()
    chunk(1, 0, 4)
    x_halo[1].wait()
    chunk(2, nx - 4, nx)
    for c in pending:
        c.wait()

    total = jnp.zeros((rows_all, rows_all), jnp.float32)
    for y in range(0, share, 2):
        a = jnp.concatenate([ufull[pl.ds(y + q, rows_all, stride=share), :] for q in range(2)], axis=1)
        total = total + lax.dot_general(
            a, a, (((1,), (1,)), ((), ())), precision=HIGHEST, preferred_element_type=jnp.float32
        )
    rows = nx * kinds
    gpart[...] = total.reshape(count_x, rows, rows_all)
    copies = []
    for k in range(1, count_x):
        to = peer("gx", k)
        copies.append(send(gpart.at[to["gx"]], garecv.at[k - 1], gas.at[k - 1], gar.at[k - 1], to))
    block = gpart[me_x]
    for k, c in enumerate(copies):
        c.wait()
        block = block + garecv[k]
    width = rows_all // count_z
    for k in range(count_z):
        gbsend[k] = block[:, k * width : (k + 1) * width]
    copies = []
    for k in range(1, count_z):
        to = peer("gz", k)
        copies.append(send(gbsend.at[to["gz"]], gbrecv.at[k - 1], gbs.at[k - 1], gbr.at[k - 1], to))
    block = gbsend[here["gz"]]
    for k, c in enumerate(copies):
        c.wait()
        block = block + gbrecv[k]
    me_y = here["gy"]
    gcall[me_y] = block
    copies = [
        send(gcall.at[me_y], gcall.at[me_y], gcs.at[k - 1], gcr.at[k - 1], peer("gy", k)) for k in range(1, count_y)
    ]
    for c in copies:
        c.wait()
    block = gcall[0]
    for k in range(1, count_y):
        block = block + gcall[k]
    gram[...] = block / columns_all
    for c in outs:
        c.wait()


def body(sizes, species, velocity, diffusivity, reaction):
    count_x, count_y, count_z = sizes
    kinds, nx, ny, lanes = species.shape
    rows = nx * kinds
    rows_all = rows * count_x
    width = rows_all // count_z
    columns_all = float(ny * lanes * count_y * count_z)
    most = max(sizes)
    f32 = jnp.float32
    vm = lambda *shape: pltpu.VMEM(shape, f32)
    dma = pltpu.SemaphoreType.DMA
    hbm = pl.BlockSpec(memory_space=pl.ANY)
    vmem = pl.BlockSpec(memory_space=pltpu.VMEM)
    smem = pl.BlockSpec(memory_space=pltpu.SMEM)
    return pl.pallas_call(
        functools.partial(kernel, sizes, columns_all),
        out_shape=(
            jax.ShapeDtypeStruct(species.shape, f32),
            jax.ShapeDtypeStruct((rows, width), f32),
        ),
        in_specs=[hbm, hbm, hbm, smem, vmem],
        out_specs=(hbm, vmem),
        scratch_shapes=[
            vm(kinds, nx + 8, ny + 16, lanes),
            vm(3, nx, ny, lanes),
            vm(nx, ny, lanes),
            vm(kinds, nx, ny, lanes),
            vm(kinds, nx, ny, lanes),
            vm(count_x, rows * ny // count_x, lanes),
            vm(rows * ny, lanes),
            vm(kinds * ny, lanes),
            vm(2, kinds * ny, lanes),
            vm(3, 8, lanes),
            vm(3, most - 1, 8, lanes),
            vm(count_x, rows, rows_all),
            vm(count_x - 1, rows, rows_all),
            vm(count_z, rows, width),
            vm(count_z - 1, rows, width),
            vm(count_y, rows, width),
            dma((3,)), dma((3,)), dma((3,)),
            dma((6,)), dma((6,)),
            dma((3, most - 1)), dma((3, most - 1)),
            dma((3, count_x - 1)), dma((3, count_x - 1)),
            dma((count_x - 1,)), dma((count_x - 1,)),
            dma((count_z - 1,)), dma((count_z - 1,)),
            dma((count_y - 1,)), dma((count_y - 1,)),
        ],
        compiler_params=pltpu.CompilerParams(
            collective_id=0, has_side_effects=True, vmem_limit_bytes=40 * 1024 * 1024
        ),
    )(species, velocity, diffusivity, reaction, jnp.asarray(lane_matrix(lanes)))


def solution(mesh):
    sizes = tuple(mesh.shape[a] for a in ("gx", "gy", "gz"))
    placed = (P(None, "gx", "gy", "gz"), P(None, "gx", "gy", "gz"), P("gx", "gy", "gz"), P())
    return jax.shard_map(
        functools.partial(body, sizes),
        mesh=mesh,
        in_specs=placed,
        out_specs=(P(None, "gx", "gy", "gz"), P("gx", "gz")),
        check_vma=False,
    )
```

time: 191 us -> 55.3 us (0.29)
  blocking collectives: 60.1 us -> 0 us
  waiting for transfers between devices: 57.3 us -> 0 us
  Pallas kernels: 0 us -> 47.8 us
  matrix products: 20.1 us -> 0 us
  local copies, waits for them, and re-layouts: 21.2 us -> 6.52 us
  between operations: 14.9 us -> 0.65 us
  other arithmetic: 8.58 us -> 0 us
  starting transfers between devices: 8.58 us -> 0 us
    pallas_call x0 -> x1, Pallas kernels: none -> 47.8 us  [body(): pl.pallas_call(functools.partial(kernel, sizes, columns_all), out_shape=(...]
    pmax x1 -> x0, blocking collectives: 40.5 us -> none  [body(): fastest = lax.pmax(local_speed, ('gx', 'gy', 'gz'))]
    all_gather x1 -> x0, waiting for transfers between devices: 33.7 us -> none  [body(): lax.all_gather(unfolding, 'gx', axis=0, tiled=True)]
    dot_general x2 -> x0, matrix products: 20.1 us -> none  [the longest x1 13.3 us: body(): jnp.einsum('kj,jxyz->kxyz', reaction, species, precision=lax.Precision.HI...]
    psum x1 -> x0, blocking collectives: 19.6 us -> none  [body(): summed = lax.psum(column_part, 'gy')]
    ppermute x6 -> x0, waiting for transfers between devices: 14.7 us -> none  [the longest x3 8.58 us: extended(): before = lax.ppermute(last, axis, up)]
    reduce_scatter x1 -> x0, waiting for transfers between devices: 8.93 us -> none  [body(): lax.psum_scatter(partial_gram, 'gz', scatter_dimension=1, tiled=True)]
    slice x5 -> x0, local copies, waits for them, and re-layouts: 8.76 us -> none  [the longest x3 6.65 us: extended(): initial = lax.slice_in_dim(x, 0, width, axis=dim)]
  transfers between devices with their start and end apart: 8 -> 0, of which waited for: 6 -> 0; matrix products, arithmetic and copies ran while one was open for 5% -> 0% of each run, Pallas kernels for 0% -> 0%
where the time goes in v1:
time: 55.3 us; the launch traced here: 55 us
  Pallas kernels  47.8 us (86%)
  local copies, waits for them, and re-layouts  6.52 us (12%)
  between operations  0.65 us (1%)
    pallas_call x1, Pallas kernels, body(): pl.pallas_call(functools.partial(kernel, sizes, columns_all), out_shape=(...  47.8 us
    unnamed x12, local copies, waits for them, and re-layouts  6.52 us

profile of v1, /device:TPU:0, one launch (start us, length us, event | category | flops | bytes accessed | tf_op | source)
XLA Modules:
  0.0 55.0 jit_solution(1591175855297733698)
XLA Ops:
  0.6 0.0 copy-start
  0.6 1.2 %copy-done = f32[4,16,32,128]{3,2,1,0:T(8,128)S(1)} copy-done((f32[4,16,32,128]{3,2,1,0:T(8,128)S(1)}, f32[4,16,32,128]{3,2,1,0:T(8,128)}, u32[]{:S(2)}) %copy-start) | copy-done | bytes 1048600
  1.9 0.0 copy-start.1
  1.9 1.1 %copy-done.1 = f32[3,16,32,128]{3,2,1,0:T(8,128)S(1)} copy-done((f32[3,16,32,128]{3,2,1,0:T(8,128)S(1)}, f32[3,16,32,128]{3,2,1,0:T(8,128)}, u32[]{:S(2)}) %copy-start.1) | copy-done | bytes 786456
  3.0 0.0 copy-start.2
  3.0 0.9 %copy-done.2 = f32[16,32,128]{2,1,0:T(8,128)S(1)} copy-done((f32[16,32,128]{2,1,0:T(8,128)S(1)}, f32[16,32,128]{2,1,0:T(8,128)}, u32[]{:S(2)}) %copy-start.2) | copy-done | bytes 262168
  3.9 0.0 copy-start.3
  3.9 0.9 %copy-done.3 = f32[256,256]{1,0:T(8,128)S(1)} copy-done((f32[256,256]{1,0:T(8,128)S(1)}, f32[256,256]{1,0:T(8,128)}, u32[]{:S(2)}) %copy-start.3) | copy-done | bytes 262168
  4.9 0.0 copy-start.4
  4.9 0.7 %copy-done.4 = f32[4,4]{1,0:T(4,128)S(1)} copy-done((f32[4,4]{1,0:T(4,128)S(1)}, f32[4,4]{1,0:T(4,128)}, u32[]{:S(2)}) %copy-start.4) | copy-done | bytes 88
  5.6 47.8 %shard_map.68 = (f32[4,16,32,128]{3,2,1,0:T(8,128)S(1)}, f32[64,128]{1,0:T(8,128)S(1)}) custom-call(f32[4,16,32,128]{3,2,1,0:T(8,128)S(1)} %copy-done, f32[3,16,32,128]{3,2,1,0:T(8,128)S(1)} %copy-done.1, f32[16,32,128]{2,1,0:T(8,128)S(1)} %copy-done.2, f32[4,4]{1,0:T(4,128)S(1)} %copy-done.4, f32[256,256]{1,0:T(8,128)S(1)} %copy-done.3), custom_call_target="tpu_custom_call" | custom-call | tf_op jit(solution)/shard_map/pallas_call | solution.py:261
  53.4 1.0 %copy.9 = f32[4,16,32,128]{3,2,1,0:T(8,128)} copy(f32[4,16,32,128]{3,2,1,0:T(8,128)S(1)} %get-tuple-element.4) | data formatting | bytes 2097152
  54.4 0.6 %copy.10 = f32[64,128]{1,0:T(8,128)} copy(f32[64,128]{1,0:T(8,128)S(1)} %get-tuple-element.5) | data formatting | bytes 65536
Async XLA Ops:
  0.6 1.2 %copy-start = (f32[4,16,32,128]{3,2,1,0:T(8,128)S(1)}, f32[4,16,32,128]{3,2,1,0:T(8,128)}, u32[]{:S(2)}) copy-start(f32[4,16,32,128]{3,2,1,0:T(8,128)} %sp.1) | copy-start | bytes 3145732
  1.9 1.1 %copy-start.1 = (f32[3,16,32,128]{3,2,1,0:T(8,128)S(1)}, f32[3,16,32,128]{3,2,1,0:T(8,128)}, u32[]{:S(2)}) copy-start(f32[3,16,32,128]{3,2,1,0:T(8,128)} %vel.1) | copy-start | bytes 2359300
  3.0 0.9 %copy-start.2 = (f32[16,32,128]{2,1,0:T(8,128)S(1)}, f32[16,32,128]{2,1,0:T(8,128)}, u32[]{:S(2)}) copy-start(f32[16,32,128]{2,1,0:T(8,128)} %dif.1) | copy-start | bytes 786436
  3.9 0.9 %copy-start.3 = (f32[256,256]{1,0:T(8,128)S(1)}, f32[256,256]{1,0:T(8,128)}, u32[]{:S(2)}) copy-start(f32[256,256]{1,0:T(8,128)} %constant.2.clone.lane_mat) | copy-start | bytes 786436
  4.9 0.7 %copy-start.4 = (f32[4,4]{1,0:T(4,128)S(1)}, f32[4,4]{1,0:T(4,128)}, u32[]{:S(2)}) copy-start(f32[4,4]{1,0:T(4,128)} %reac.1) | copy-start | bytes 196

commit v2 on v1

--- a/solution.py
+++ b/solution.py
@@ -31,10 +31,10 @@
 
 
 def kernel(
-    sizes, columns_all, sp, vel, dif, reac, lane_mat, out, gram,
-    pad, v, d, tend, uout, usend, ufull, zsend, zrecv, msend, mrecv,
-    gpart, garecv, gbsend, gbrecv, gcall,
-    load_sem, out_sem, own_sem, hs, hr, ms, mr, us, ur, gas, gar, gbs, gbr, gcs, gcr,
+    sizes, columns_all, sp, vel, dif, reac_in, lane_in, out, gram,
+    pad, v, d, reac, lane_mat, tend, uout, usend, ufull, zsend, zrecv, msend, mrecv,
+    gpart, garecv, gcall,
+    load_sem, out_sem, own_sem, hs, hr, ms, mr, us, ur, gas, gar, gcs, gcr,
 ):
     count_x, count_y, count_z = sizes
     kinds, nx, ny, lanes = sp.shape
@@ -44,6 +44,14 @@
     def peer(axis, step):
         n = sizes[axes.index(axis)]
         return {axis: lax.rem(here[axis] + step + n, n)}
+
+    others = [(i, k) for i in range(count_x) for k in range(count_z) if i or k]
+
+    def across(i, k):
+        return {"gx": lax.rem(here["gx"] + i, count_x), "gz": lax.rem(here["gz"] + k, count_z)}
+
+    plane = [across(i, k) for i, k in others]
+    line = [peer("gy", k) for k in range(1, count_y)]
 
     def send(src, dst, s, r, device):
         copy = pltpu.make_async_remote_copy(
@@ -53,17 +61,18 @@
         return copy
 
     barrier = pltpu.get_barrier_semaphore()
-    for axis, n in zip(axes, sizes):
-        for step in range(1, n):
-            pl.semaphore_signal(barrier, inc=1, device_id=peer(axis, step), device_id_type=MESH)
+    for to in plane + line:
+        pl.semaphore_signal(barrier, inc=1, device_id=to, device_id_type=MESH)
     loads = [
         pltpu.make_async_copy(vel, v, load_sem.at[0]),
         pltpu.make_async_copy(sp, pad.at[:, 4 : 4 + nx, 8 : 8 + ny, :], load_sem.at[1]),
         pltpu.make_async_copy(dif, d, load_sem.at[2]),
+        pltpu.make_async_copy(reac_in, reac, load_sem.at[3]),
+        pltpu.make_async_copy(lane_in, lane_mat, load_sem.at[4]),
     ]
     for c in loads:
         c.start()
-    pl.semaphore_wait(barrier, count_x + count_y + count_z - 3)
+    pl.semaphore_wait(barrier, len(plane) + len(line))
 
     x_halo = [
         send(sp.at[:, nx - 4 :], pad.at[:, 0:4, 8 : 8 + ny, :], hs.at[0], hr.at[0], peer("gx", 1)),
@@ -83,11 +92,10 @@
     most = lax.fori_loop(0, nx, speed, jnp.zeros((8, lanes), jnp.float32))
 
     def max_start(stage, value):
-        n = sizes[stage]
         msend[stage] = value
         return [
-            send(msend.at[stage], mrecv.at[stage, k - 1], ms.at[stage, k - 1], mr.at[stage, k - 1], peer(axes[stage], k))
-            for k in range(1, n)
+            send(msend.at[stage], mrecv.at[stage, k], ms.at[stage, k], mr.at[stage, k], to)
+            for k, to in enumerate((plane, line)[stage])
         ]
 
     def max_end(stage, value, copies):
@@ -111,10 +119,11 @@
     if count_z > 2:
         z_halo.append(send(zsend, zrecv.at[1], hs.at[5], hr.at[5], peer("gz", -1)))
 
+    for c in loads[2:]:
+        c.wait()
     most = max_end(0, most, stage_copies)
     stage_copies = max_start(1, most)
 
-    loads[2].wait()
     for c in z_halo:
         c.wait()
     if count_z > 2:
@@ -122,8 +131,6 @@
         zsend[...] = jnp.where(wide < 4, zrecv[0], zrecv[1])
     else:
         zsend[...] = zrecv[0]
-    most = max_end(1, most, stage_copies)
-    stage_copies = max_start(2, most)
     for c in y_halo:
         c.wait()
 
@@ -149,9 +156,8 @@
             tend[k, x] = t
         return carry
 
-    lax.fori_loop(0, nx, rest, 0)
-
-    most = max_end(2, most, stage_copies)
+    lax.fori_loop(4, nx - 4, rest, 0)
+    most = max_end(1, most, stage_copies)
     fastest = jnp.max(most, keepdims=True)
     dt = jnp.broadcast_to(courant / fastest, (ny, lanes))
 
@@ -195,8 +201,10 @@
         outs.append(keep)
 
     chunk(0, 4, nx - 4)
+    lax.fori_loop(0, 4, rest, 0)
     x_halo[0].wait()
     chunk(1, 0, 4)
+    lax.fori_loop(nx - 4, nx, rest, 0)
     x_halo[1].wait()
     chunk(2, nx - 4, nx)
     for c in pending:
@@ -209,30 +217,20 @@
             a, a, (((1,), (1,)), ((), ())), precision=HIGHEST, preferred_element_type=jnp.float32
         )
     rows = nx * kinds
-    gpart[...] = total.reshape(count_x, rows, rows_all)
-    copies = []
-    for k in range(1, count_x):
-        to = peer("gx", k)
-        copies.append(send(gpart.at[to["gx"]], garecv.at[k - 1], gas.at[k - 1], gar.at[k - 1], to))
-    block = gpart[me_x]
-    for k, c in enumerate(copies):
-        c.wait()
-        block = block + garecv[k]
     width = rows_all // count_z
     for k in range(count_z):
-        gbsend[k] = block[:, k * width : (k + 1) * width]
-    copies = []
-    for k in range(1, count_z):
-        to = peer("gz", k)
-        copies.append(send(gbsend.at[to["gz"]], gbrecv.at[k - 1], gbs.at[k - 1], gbr.at[k - 1], to))
-    block = gbsend[here["gz"]]
+        gpart[:, k] = total[:, k * width : (k + 1) * width].reshape(count_x, rows, width)
+    copies = [
+        send(gpart.at[to["gx"], to["gz"]], garecv.at[k], gas.at[k], gar.at[k], to) for k, to in enumerate(plane)
+    ]
+    block = gpart[me_x, here["gz"]]
     for k, c in enumerate(copies):
         c.wait()
-        block = block + gbrecv[k]
+        block = block + garecv[k]
     me_y = here["gy"]
     gcall[me_y] = block
     copies = [
-        send(gcall.at[me_y], gcall.at[me_y], gcs.at[k - 1], gcr.at[k - 1], peer("gy", k)) for k in range(1, count_y)
+        send(gcall.at[me_y], gcall.at[me_y], gcs.at[k], gcr.at[k], to) for k, to in enumerate(line)
     ]
     for c in copies:
         c.wait()
@@ -242,6 +240,26 @@
     gram[...] = block / columns_all
     for c in outs:
         c.wait()
+
+
+def place(a, b, out_a, out_b, hold_a, hold_b, sems, sem):
+    kinds, nx = a.shape[:2]
+    half = nx // 2
+    pairs = [
+        (
+            pltpu.make_async_copy(a.at[k, part], hold_a.at[k, part], sems.at[i]),
+            pltpu.make_async_copy(hold_a.at[k, part], out_a.at[k, part], sems.at[2 * kinds + i]),
+        )
+        for i, (k, part) in enumerate((k, pl.ds(h * half, half)) for k in range(kinds) for h in range(2))
+    ]
+    pairs.append((pltpu.make_async_copy(b, hold_b, sem.at[0]), pltpu.make_async_copy(hold_b, out_b, sem.at[1])))
+    for c, _ in pairs:
+        c.start()
+    for c, e in pairs:
+        c.wait()
+        e.start()
+    for _, e in pairs:
+        e.wait()
 
 
 def body(sizes, species, velocity, diffusivity, reaction):
@@ -251,50 +269,56 @@
     rows_all = rows * count_x
     width = rows_all // count_z
     columns_all = float(ny * lanes * count_y * count_z)
-    most = max(sizes)
+    plane = count_x * count_z - 1
+    most = max(plane, count_y - 1)
     f32 = jnp.float32
     vm = lambda *shape: pltpu.VMEM(shape, f32)
     dma = pltpu.SemaphoreType.DMA
     hbm = pl.BlockSpec(memory_space=pl.ANY)
     vmem = pl.BlockSpec(memory_space=pltpu.VMEM)
-    smem = pl.BlockSpec(memory_space=pltpu.SMEM)
-    return pl.pallas_call(
+    got = pl.pallas_call(
         functools.partial(kernel, sizes, columns_all),
         out_shape=(
             jax.ShapeDtypeStruct(species.shape, f32),
             jax.ShapeDtypeStruct((rows, width), f32),
         ),
-        in_specs=[hbm, hbm, hbm, smem, vmem],
+        in_specs=[hbm] * 5,
         out_specs=(hbm, vmem),
         scratch_shapes=[
             vm(kinds, nx + 8, ny + 16, lanes),
             vm(3, nx, ny, lanes),
             vm(nx, ny, lanes),
+            pltpu.SMEM((kinds, kinds), f32),
+            vm(2 * lanes, 2 * lanes),
             vm(kinds, nx, ny, lanes),
             vm(kinds, nx, ny, lanes),
             vm(count_x, rows * ny // count_x, lanes),
             vm(rows * ny, lanes),
             vm(kinds * ny, lanes),
             vm(2, kinds * ny, lanes),
-            vm(3, 8, lanes),
-            vm(3, most - 1, 8, lanes),
-            vm(count_x, rows, rows_all),
-            vm(count_x - 1, rows, rows_all),
-            vm(count_z, rows, width),
-            vm(count_z - 1, rows, width),
+            vm(2, 8, lanes),
+            vm(2, most, 8, lanes),
+            vm(count_x, count_z, rows, width),
+            vm(plane, rows, width),
             vm(count_y, rows, width),
-            dma((3,)), dma((3,)), dma((3,)),
+            dma((5,)), dma((3,)), dma((3,)),
             dma((6,)), dma((6,)),
-            dma((3, most - 1)), dma((3, most - 1)),
+            dma((2, most)), dma((2, most)),
             dma((3, count_x - 1)), dma((3, count_x - 1)),
-            dma((count_x - 1,)), dma((count_x - 1,)),
-            dma((count_z - 1,)), dma((count_z - 1,)),
+            dma((plane,)), dma((plane,)),
             dma((count_y - 1,)), dma((count_y - 1,)),
         ],
         compiler_params=pltpu.CompilerParams(
-            collective_id=0, has_side_effects=True, vmem_limit_bytes=40 * 1024 * 1024
+            collective_id=0, has_side_effects=True, vmem_limit_bytes=60 * 1024 * 1024
         ),
     )(species, velocity, diffusivity, reaction, jnp.asarray(lane_matrix(lanes)))
+    return pl.pallas_call(
+        place,
+        out_shape=tuple(jax.ShapeDtypeStruct(g.shape, f32) for g in got),
+        in_specs=[hbm] * 2,
+        out_specs=(hbm, hbm),
+        scratch_shapes=[vm(*got[0].shape), vm(*got[1].shape), dma((4 * kinds,)), dma((2,))],
+    )(*got)
 
 
 def solution(mesh):

time: 55.3 us -> 44.5 us (0.80)
  local copies, waits for them, and re-layouts: 6.52 us -> 0 us
  Pallas kernels: 47.8 us -> 43.8 us
    unnamed x12 -> x0, local copies, waits for them, and re-layouts: 6.52 us -> none
    pallas_call x1, Pallas kernels: 47.8 us -> 41.6 us  [body(): pl.pallas_call(functools.partial(kernel, sizes, columns_all), out_shape=(...]
    pallas_call x0 -> x1, Pallas kernels: none -> 2.11 us  [body(): pl.pallas_call(place, out_shape=tuple((jax.ShapeDtypeStruct(g.shape, f32)...]
where the time goes in v2:
time: 44.5 us; the launch traced here: 44.4 us
  Pallas kernels  43.8 us (98%)
  between operations  0.64 us (1%)
    pallas_call x1, Pallas kernels, body(): pl.pallas_call(functools.partial(kernel, sizes, columns_all), out_shape=(...  41.6 us
    pallas_call x1, Pallas kernels, body(): pl.pallas_call(place, out_shape=tuple((jax.ShapeDtypeStruct(g.shape, f32)...  2.11 us

profile of v2, /device:TPU:0, one launch (start us, length us, event | category | flops | bytes accessed | tf_op | source)
XLA Modules:
  0.0 44.4 jit_solution(962299632040609770)
XLA Ops:
  0.6 41.6 %shard_map.68 = (f32[4,16,32,128]{3,2,1,0:T(8,128)}, f32[64,128]{1,0:T(8,128)}) custom-call(f32[4,16,32,128]{3,2,1,0:T(8,128)} %sp.1, f32[3,16,32,128]{3,2,1,0:T(8,128)} %vel.1, f32[16,32,128]{2,1,0:T(8,128)} %dif.1, f32[4,4]{1,0:T(4,128)} %reac_in.1, f32[256,256]{1,0:T(8,128)} %constant.2.clone.lane_in), custom_call_target="tpu_custom_call" | custom-call | tf_op jit(solution)/shard_map/pallas_call | solution.py:279
  42.3 2.1 %shard_map.69 = (f32[4,16,32,128]{3,2,1,0:T(8,128)}, f32[64,128]{1,0:T(8,128)}) custom-call(f32[4,16,32,128]{3,2,1,0:T(8,128)} %get-tuple-element.4.a, f32[64,128]{1,0:T(8,128)} %get-tuple-element.5.b), custom_call_target="tpu_custom_call" | custom-call | tf_op jit(solution)/shard_map/pallas_call | solution.py:315

commit v3 on v2

--- a/solution.py
+++ b/solution.py
@@ -64,9 +64,12 @@
     for to in plane + line:
         pl.semaphore_signal(barrier, inc=1, device_id=to, device_id_type=MESH)
     loads = [
-        pltpu.make_async_copy(vel, v, load_sem.at[0]),
-        pltpu.make_async_copy(sp, pad.at[:, 4 : 4 + nx, 8 : 8 + ny, :], load_sem.at[1]),
-        pltpu.make_async_copy(dif, d, load_sem.at[2]),
+        *(pltpu.make_async_copy(vel.at[i], v.at[i], load_sem.at[i]) for i in range(3)),
+        *(
+            pltpu.make_async_copy(sp.at[k], pad.at[k, 4 : 4 + nx, 8 : 8 + ny, :], load_sem.at[5 + k])
+            for k in range(kinds)
+        ),
+        pltpu.make_async_copy(dif, d, load_sem.at[5 + kinds]),
         pltpu.make_async_copy(reac_in, reac, load_sem.at[3]),
         pltpu.make_async_copy(lane_in, lane_mat, load_sem.at[4]),
     ]
@@ -83,7 +86,8 @@
         send(sp.at[:, :, 0:4], pad.at[:, 4 : 4 + nx, 8 + ny : 12 + ny, :], hs.at[3], hr.at[3], peer("gy", -1)),
     ]
 
-    loads[0].wait()
+    for c in loads[:3]:
+        c.wait()
 
     def speed(x, m):
         s = jnp.abs(v[0, x]) + jnp.abs(v[1, x]) + jnp.abs(v[2, x])
@@ -106,7 +110,8 @@
 
     stage_copies = max_start(0, most)
 
-    loads[1].wait()
+    for c in loads[3 : 3 + kinds]:
+        c.wait()
     lane = lax.broadcasted_iota(jnp.int32, (kinds * ny, lanes), 1)
     edge = (lane < 4) | (lane >= lanes - 4)
 
@@ -119,7 +124,7 @@
     if count_z > 2:
         z_halo.append(send(zsend, zrecv.at[1], hs.at[5], hr.at[5], peer("gz", -1)))
 
-    for c in loads[2:]:
+    for c in loads[3 + kinds :]:
         c.wait()
     most = max_end(0, most, stage_copies)
     stage_copies = max_start(1, most)
@@ -188,7 +193,7 @@
         rows = pl.ds(low * kinds * share, (high - low) * kinds * share)
         start = pl.multiple_of(me_x * (nx * kinds * share) + low * kinds * share, share)
         there = ufull.at[pl.ds(start, (high - low) * kinds * share)]
-        for k in range(1, count_x):
+        for k in sorted(range(1, count_x), key=lambda k: abs(2 * k - count_x)):
             to = peer("gx", k)
             pending.append(
                 send(usend.at[to["gx"], rows], there, us.at[index, k - 1], ur.at[index, k - 1], to)
@@ -213,31 +218,47 @@
     total = jnp.zeros((rows_all, rows_all), jnp.float32)
     for y in range(0, share, 2):
         a = jnp.concatenate([ufull[pl.ds(y + q, rows_all, stride=share), :] for q in range(2)], axis=1)
-        total = total + lax.dot_general(
-            a, a, (((1,), (1,)), ((), ())), precision=HIGHEST, preferred_element_type=jnp.float32
-        )
+        big = a.astype(jnp.bfloat16)
+        small = (a - big.astype(jnp.float32)).astype(jnp.bfloat16)
+        for left, right in ((big, big), (big, small), (small, big)):
+            total = total + lax.dot_general(
+                left, right, (((1,), (1,)), ((), ())), preferred_element_type=jnp.float32
+            )
     rows = nx * kinds
     width = rows_all // count_z
     for k in range(count_z):
         gpart[:, k] = total[:, k * width : (k + 1) * width].reshape(count_x, rows, width)
-    copies = [
-        send(gpart.at[to["gx"], to["gz"]], garecv.at[k], gas.at[k], gar.at[k], to) for k, to in enumerate(plane)
-    ]
-    block = gpart[me_x, here["gz"]]
-    for k, c in enumerate(copies):
-        c.wait()
-        block = block + garecv[k]
-    me_y = here["gy"]
-    gcall[me_y] = block
-    copies = [
-        send(gcall.at[me_y], gcall.at[me_y], gcs.at[k], gcr.at[k], to) for k, to in enumerate(line)
-    ]
-    for c in copies:
-        c.wait()
-    block = gcall[0]
-    for k in range(1, count_y):
-        block = block + gcall[k]
-    gram[...] = block / columns_all
+    pieces = 2
+    size = rows // pieces
+    parts = [pl.ds(h * size, size) for h in range(pieces)]
+    first_sends = [
+        [
+            send(gpart.at[to["gx"], to["gz"], part], garecv.at[k, part], gas.at[h, k], gar.at[h, k], to)
+            for k, to in enumerate(plane)
+        ]
+        for h, part in enumerate(parts)
+    ]
+    me_y, me_z = here["gy"], here["gz"]
+    last_sends = []
+    for h, part in enumerate(parts):
+        block = gpart[me_x, me_z, part]
+        for k, c in enumerate(first_sends[h]):
+            c.wait()
+            block = block + garecv[k, part]
+        gcall[me_y, part] = block
+        last_sends.append(
+            [
+                send(gcall.at[me_y, part], gcall.at[me_y, part], gcs.at[h, k], gcr.at[h, k], to)
+                for k, to in enumerate(line)
+            ]
+        )
+    for h, part in enumerate(parts):
+        for c in last_sends[h]:
+            c.wait()
+        block = gcall[0, part]
+        for k in range(1, count_y):
+            block = block + gcall[k, part]
+        gram[part] = block / columns_all
     for c in outs:
         c.wait()
 
@@ -301,12 +322,12 @@
             vm(count_x, count_z, rows, width),
             vm(plane, rows, width),
             vm(count_y, rows, width),
-            dma((5,)), dma((3,)), dma((3,)),
+            dma((6 + kinds,)), dma((3,)), dma((3,)),
             dma((6,)), dma((6,)),
             dma((2, most)), dma((2, most)),
             dma((3, count_x - 1)), dma((3, count_x - 1)),
-            dma((plane,)), dma((plane,)),
-            dma((count_y - 1,)), dma((count_y - 1,)),
+            dma((2, plane)), dma((2, plane)),
+            dma((2, count_y - 1)), dma((2, count_y - 1)),
         ],
         compiler_params=pltpu.CompilerParams(
             collective_id=0, has_side_effects=True, vmem_limit_bytes=60 * 1024 * 1024

time: 44.5 us -> 43.9 us (0.987)
  Pallas kernels: 43.8 us -> 43.1 us
    pallas_call x1, Pallas kernels: 41.6 us -> 41 us  [body(): pl.pallas_call(functools.partial(kernel, sizes, columns_all), out_shape=(...]
where the time goes in v3:
time: 43.9 us; the launch traced here: 43.8 us
  Pallas kernels  43.1 us (98%)
  between operations  0.64 us (1%)
    pallas_call x1, Pallas kernels, body(): pl.pallas_call(functools.partial(kernel, sizes, columns_all), out_shape=(...  41 us
    pallas_call x1, Pallas kernels, body(): pl.pallas_call(place, out_shape=tuple((jax.ShapeDtypeStruct(g.shape, f32)...  2.11 us

profile of v3, /device:TPU:0, one launch (start us, length us, event | category | flops | bytes accessed | tf_op | source)
XLA Modules:
  0.0 43.8 jit_solution(18154397790387975680)
XLA Ops:
  0.6 41.0 %shard_map.68 = (f32[4,16,32,128]{3,2,1,0:T(8,128)}, f32[64,128]{1,0:T(8,128)}) custom-call(f32[4,16,32,128]{3,2,1,0:T(8,128)} %sp.1, f32[3,16,32,128]{3,2,1,0:T(8,128)} %vel.1, f32[16,32,128]{2,1,0:T(8,128)} %dif.1, f32[4,4]{1,0:T(4,128)} %reac_in.1, f32[256,256]{1,0:T(8,128)} %constant.2.clone.lane_in), custom_call_target="tpu_custom_call" | custom-call | tf_op jit(solution)/shard_map/pallas_call | solution.py:300
  41.7 2.1 %shard_map.69 = (f32[4,16,32,128]{3,2,1,0:T(8,128)}, f32[64,128]{1,0:T(8,128)}) custom-call(f32[4,16,32,128]{3,2,1,0:T(8,128)} %get-tuple-element.4.a, f32[64,128]{1,0:T(8,128)} %get-tuple-element.5.b), custom_call_target="tpu_custom_call" | custom-call | tf_op jit(solution)/shard_map/pallas_call | solution.py:336
